TPU v7x, 32 devices: a whole 2x2x4 slice. The times are simulated.
32 devices in a mesh: rows: 8 (over z, y), snaps: 4 (over x, core).
Axes of the slice: x: 2, y: 2, z: 4, core: 2. Of those that a mesh axis runs over, the one named last changes fastest.
Arguments:
- stress: float32 [131072, 1024], P('rows', 'snaps'), may hold values from -80 to 80
- sketch: float32 [64, 1024], P(None, 'snaps'), may hold values from -0.1875 to 0.1875
Outputs:
- basis: float32 [64, 131072], P(None, ('rows', 'snaps'))
- coeffs: float32 [64, 1024], P(None, 'snaps')
- spectrum: float32 [64, 64], replicated
All inputs are finite; a program needn't handle non-finite values.
Results may differ from a plain program's by a relative error of at most 0.0015.
Values sent between devices are 32-bit elements; how exact they have to be, the bound alone decides.
A program may use at most 128 MiB of HBM per device.

v0:
```python
import math
import jax
import jax.numpy as jnp
from jax import lax
from jax.sharding import PartitionSpec as P


def product(left_m, right_m, left_dim, right_dim):
    return lax.dot_general(
        left_m,
        right_m,
        (((left_dim,), (right_dim,)), ((), ())),
        precision=lax.Precision.HIGHEST,
        preferred_element_type=jnp.float32,
    )


def inverse_factor(gram_total):
    lower = jnp.linalg.cholesky(gram_total)
    ident = jnp.eye(gram_total.shape[0], dtype=gram_total.dtype)
    return lax.linalg.triangular_solve(lower, ident, left_side=True, lower=True)


def section_whole(panel, stress):
    factor = inverse_factor(lax.psum(product(panel, panel, 1, 1), "rows"))
    basis = product(factor, panel, 1, 0)
    coeffs = lax.psum(product(basis, stress, 1, 0), "rows")
    return (basis, coeffs)


def on_device(stress, sketch):
    rows_dev = stress.shape[0]
    groups = lax.axis_size("snaps")
    share = rows_dev // groups
    operand = sketch
    basis = None
    for turn in range(2):
        partial_value = product(operand, stress, 1, 1)
        panel = lax.psum(partial_value, "snaps")
        basis, operand = section_whole(panel, stress)
    basis = lax.dynamic_slice_in_dim(basis, lax.axis_index("snaps") * share, share, 1)
    scale = math.sqrt(float(rows_dev * lax.axis_size("rows")))
    batch_total = operand.shape[1] * groups
    spectrum = lax.psum(product(operand, operand, 1, 1), "snaps") / batch_total
    return (basis * scale, operand, spectrum)


def solution(mesh):
    placed = (P("rows", "snaps"), P(None, "snaps"))
    return jax.shard_map(
        on_device,
        mesh=mesh,
        in_specs=placed,
        out_specs=(P(None, ("rows", "snaps")), P(None, "snaps"), P()),
        check_vma=False,
    )
```

profile of v0, /device:TPU:0, one launch (start us, length us, event | category | flops | bytes accessed | tf_op | source)
XLA Modules:
  0.0 522.6 jit_solution(17021512674975102727)
XLA Ops:
  7.2 0.0 copy-start
  7.2 0.0 all-reduce.5.cloned.1.call-start
  7.2 0.8 copy-done
  8.0 20.6 %fusion.12 = f32[64,16384]{1,0:T(8,128)} fusion(f32[64,256]{1,0:T(8,128)S(1)} %copy-done, f32[16384,256]{1,0:T(8,128)} %param.5), kind=kOutput, calls=%fused_computation.23 | convolution fusion | flops 3221225472 | bytes 21037056 | tf_op jit(solution)/shard_map/dot_general | solution.py:9
  28.6 0.0 all-reduce.5.cloned.1.call-update
  28.7 0.0 all-reduce.7.cloned.1.call-start
  28.7 88.3 %all-reduce.5.cloned.1.call-done = f32[64,16384]{1,0:T(8,128)} async-done(((f32[64,16384]{1,0:T(8,128)}), f32[64,16384]{1,0:T(8,128)}) %all-reduce.5.cloned.1.call-update) | async-done | bytes 4194320 | tf_op jit(solution)/shard_map/psum | solution.py:39
  117.0 6.9 %fusion.13 = f32[64,64]{0,1:T(8,128)S(1)} fusion(f32[64,16384]{1,0:T(8,128)} %all-reduce.5.cloned.1.call-done), kind=kOutput, calls=%fused_computation.24 | convolution fusion | flops 805306368 | bytes 4210688 | tf_op jit(solution)/shard_map/dot_general | solution.py:9
  124.0 37.2 %psum.50 = f32[64,64]{0,1:T(8,128)S(1)} all-reduce(f32[64,64]{0,1:T(8,128)S(1)} %fusion.13), channel_id=1, replica_groups=mesh['rows'=8,'snaps'=4] {'rows'}, use_global_device_ids=true, to_apply=%region_1.0 | all-reduce | flops 4096 | bytes 32768 | tf_op jit(solution)/shard_map/psum | solution.py:25
  161.1 0.1 copy.6
  161.2 5.8 %cholesky.44 = f32[64,64]{1,0:T(8,128)S(1)} custom-call(f32[64,64]{1,0:T(8,128)S(1)} %fusion.9), custom_call_target="Cholesky" | custom-call | tf_op jit(solution)/shard_map/jit(cholesky)/cholesky | solution.py:19
  167.1 0.6 compare_reduce_fusion.1
  167.7 0.7 fusion.4
  168.4 4.9 custom-call.6
  173.3 0.3 fusion.2
  173.5 5.5 %fusion.14 = f32[64,16384]{1,0:T(8,128)S(1)} fusion(f32[64,64]{1,0:T(8,128)S(1)} %fusion.2, f32[64,16384]{1,0:T(8,128)} %all-reduce.5.cloned.1.call-done), kind=kOutput, calls=%fused_computation.25 | convolution fusion | flops 805306368 | bytes 8404992 | tf_op jit(solution)/shard_map/dot_general | solution.py:9
  179.0 11.6 %fusion.15 = f32[64,256]{1,0:T(8,128)} fusion(f32[64,16384]{1,0:T(8,128)S(1)} %fusion.14, f32[16384,256]{1,0:T(8,128)} %param.5), kind=kOutput, calls=%fused_computation.26 | convolution fusion | flops 3221225472 | bytes 21037056 | tf_op jit(solution)/shard_map/dot_general | solution.py:9
  190.6 0.0 all-reduce.7.cloned.1.call-update
  190.6 0.3 all-reduce.9.cloned.1.call-start
  190.9 64.8 %all-reduce.7.cloned.1.call-done = f32[64,256]{1,0:T(8,128)} async-done(((f32[64,256]{1,0:T(8,128)}), f32[64,256]{1,0:T(8,128)}) %all-reduce.7.cloned.1.call-update) | async-done | bytes 65552 | tf_op jit(solution)/shard_map/psum | solution.py:27
  255.7 20.6 %fusion.16 = f32[64,16384]{1,0:T(8,128)} fusion(f32[64,256]{1,0:T(8,128)} %all-reduce.7.cloned.1.call-done, f32[16384,256]{1,0:T(8,128)} %param.5), kind=kOutput, calls=%fused_computation.27 | convolution fusion | flops 3221225472 | bytes 21037056 | tf_op jit(solution)/shard_map/dot_general | solution.py:9
  276.3 0.0 all-reduce.9.cloned.1.call-update
  276.4 0.0 all-reduce.11.cloned.1.call-start
  276.4 85.5 %all-reduce.9.cloned.1.call-done = f32[64,16384]{1,0:T(8,128)} async-done(((f32[64,16384]{1,0:T(8,128)}), f32[64,16384]{1,0:T(8,128)}) %all-reduce.9.cloned.1.call-update) | async-done | bytes 4194320 | tf_op jit(solution)/shard_map/psum | solution.py:39
  361.9 6.9 %fusion.17 = f32[64,64]{0,1:T(8,128)S(1)} fusion(f32[64,16384]{1,0:T(8,128)} %all-reduce.9.cloned.1.call-done), kind=kOutput, calls=%fused_computation.28 | convolution fusion | flops 805306368 | bytes 4210688 | tf_op jit(solution)/shard_map/dot_general | solution.py:9
  368.9 37.1 %psum.53 = f32[64,64]{0,1:T(8,128)S(1)} all-reduce(f32[64,64]{0,1:T(8,128)S(1)} %fusion.17), channel_id=1, replica_groups=mesh['rows'=8,'snaps'=4] {'rows'}, use_global_device_ids=true, to_apply=%region_6.9 | all-reduce | flops 4096 | bytes 32768 | tf_op jit(solution)/shard_map/psum | solution.py:25
  406.0 0.1 copy.8
  406.1 5.8 %cholesky.55 = f32[64,64]{1,0:T(8,128)S(1)} custom-call(f32[64,64]{1,0:T(8,128)S(1)} %fusion.7), custom_call_target="Cholesky" | custom-call | tf_op jit(solution)/shard_map/jit(cholesky)/cholesky | solution.py:19
  412.0 0.6 compare_reduce_fusion
  412.7 0.7 fusion.5
  413.3 4.9 custom-call.7
  418.2 0.3 fusion
  418.5 5.5 %fusion.18 = f32[64,16384]{1,0:T(8,128)S(1)} fusion(f32[64,64]{1,0:T(8,128)S(1)} %fusion, f32[64,16384]{1,0:T(8,128)} %all-reduce.9.cloned.1.call-done), kind=kOutput, calls=%fused_computation.29 | convolution fusion | flops 805306368 | bytes 8404992 | tf_op jit(solution)/shard_map/dot_general | solution.py:9
  423.9 0.0 copy-start.1
  423.9 1.9 copy-done.1
  425.9 11.6 %fusion.19 = f32[64,256]{1,0:T(8,128)} fusion(f32[64,16384]{1,0:T(8,128)S(1)} %fusion.18, f32[16384,256]{1,0:T(8,128)} %param.5), kind=kOutput, calls=%fused_computation.30 | convolution fusion | flops 3221225472 | bytes 21037056 | tf_op jit(solution)/shard_map/dot_general | solution.py:9
  437.4 0.0 all-reduce.11.cloned.1.call-update
  437.5 2.3 dynamic-slice_multiply_fusion
  439.8 62.8 %all-reduce.11.cloned.1.call-done = f32[64,256]{1,0:T(8,128)} async-done(((f32[64,256]{1,0:T(8,128)}), f32[64,256]{1,0:T(8,128)}) %all-reduce.11.cloned.1.call-update) | async-done | bytes 65552 | tf_op jit(solution)/shard_map/psum | solution.py:27
  502.5 1.1 fusion.20
  503.7 10.3 %psum.55 = f32[64,64]{1,0:T(8,128)S(1)} all-reduce(f32[64,64]{1,0:T(8,128)S(1)} %fusion.20), channel_id=1, replica_groups=mesh['rows'=8,'snaps'=4] {'snaps'}, use_global_device_ids=true, to_apply=%region_8.11 | all-reduce | flops 4096 | bytes 32768 | tf_op jit(solution)/shard_map/psum | solution.py:44
  513.9 0.6 broadcast_multiply_fusion
  514.6 1.5 copy.15
  (4 shorter events, 0.1 us)
Async XLA Ops:
  7.2 0.8 copy-start
  7.2 109.8 %all-reduce.5.cloned.1.call-start = ((), (), s32[]{:S(2)}) async-start(), calls=%async_computation | async-start | bytes 8388608 | tf_op jit(solution)/shard_map/psum | solution.py:39
  28.7 227.1 %all-reduce.7.cloned.1.call-start = ((), (), s32[]{:S(2)}) async-start(), calls=%async_computation.1 | async-start | bytes 131072 | tf_op jit(solution)/shard_map/psum | solution.py:27
  190.6 171.3 %all-reduce.9.cloned.1.call-start = ((), (), s32[]{:S(2)}) async-start(), calls=%async_computation.2 | async-start | bytes 8388608 | tf_op jit(solution)/shard_map/psum | solution.py:39
  276.4 226.2 %all-reduce.11.cloned.1.call-start = ((), (), s32[]{:S(2)}) async-start(), calls=%async_computation.3 | async-start | bytes 131072 | tf_op jit(solution)/shard_map/psum | solution.py:27
  423.9 1.9 copy-start.1
Sparse Core Ops, SparseCore 0:
  28.8 88.1 all-reduce.4
  190.8 64.9 all-reduce.6
  276.5 85.4 all-reduce.8
  437.6 64.9 all-reduce.10
where the time goes:
time: 523 us
  waiting for transfers between devices  301 us (58%)
  matrix products  90.8 us (17%)
  blocking collectives  84.6 us (16%)
  other arithmetic  27.1 us (5%)
  between operations  13.9 us (3%)
    psum x2, waiting for transfers between devices, on_device(): panel = lax.psum(partial_value, 'snaps')  174 us
    psum x2, waiting for transfers between devices, section_whole(): coeffs = lax.psum(product(basis, stress, 1, 0), 'rows')  128 us
    dot_general x9, matrix products, product(): lax.dot_general(left_m, right_m, (((left_dim,), (right_dim,)), ((), ())),...  90.3 us
    psum x2, blocking collectives, section_whole(): factor = inverse_factor(lax.psum(product(panel, panel, 1, 1), 'rows'))  74.3 us
    another operation x6, other arithmetic, inverse_factor(): lower = jnp.linalg.cholesky(gram_total)  13 us
    another operation x4, other arithmetic, inverse_factor(): return lax.linalg.triangular_solve(lower, ident, left_side=True, lower=True)  11.1 us
  transfers between devices with their start and end apart: 4, of which 4 were waited for; matrix products, arithmetic and copies ran while one was open for 0% of the time, Pallas kernels for 0%

commit v1 on v0

--- a/solution.py
+++ b/solution.py
@@ -36,7 +36,7 @@
     basis = None
     for turn in range(2):
         partial_value = product(operand, stress, 1, 1)
-        panel = lax.psum(partial_value, "snaps")
+        panel = lax.all_gather(partial_value, "snaps").sum(axis=0)
         basis, operand = section_whole(panel, stress)
     basis = lax.dynamic_slice_in_dim(basis, lax.axis_index("snaps") * share, share, 1)
     scale = math.sqrt(float(rows_dev * lax.axis_size("rows")))

time: 523 us -> 603 us (1.15); the launches traced: 523 us -> 594 us
  waiting for transfers between devices: 301 us -> 342 us
  other arithmetic: 27.1 us -> 45.5 us
  blocking collectives: 84.6 us -> 96.9 us
    all_gather x0 -> x2, waiting for transfers between devices: none -> 215 us  [on_device(): panel = lax.all_gather(partial_value, 'snaps').sum(axis=0)]
    psum x2 -> x0, waiting for transfers between devices: 174 us -> none  [on_device(): panel = lax.psum(partial_value, 'snaps')]
    reduce_sum x0 -> x2, other arithmetic: none -> 18.5 us  [on_device(): panel = lax.all_gather(partial_value, 'snaps').sum(axis=0)]
    psum x2, blocking collectives: 74.3 us -> 86.7 us  [section_whole(): factor = inverse_factor(lax.psum(product(panel, panel, 1, 1), 'rows'))]
where the time goes in v1:
time: 603 us; the launch traced here: 594 us
  waiting for transfers between devices  342 us (57%)
  blocking collectives  96.9 us (16%)
  matrix products  90.9 us (15%)
  other arithmetic  45.5 us (8%)
  between operations  14.3 us (2%)
    all_gather x2, waiting for transfers between devices, on_device(): panel = lax.all_gather(partial_value, 'snaps').sum(axis=0)  215 us
    psum x2, waiting for transfers between devices, section_whole(): coeffs = lax.psum(product(basis, stress, 1, 0), 'rows')  128 us
    dot_general x9, matrix products, product(): lax.dot_general(left_m, right_m, (((left_dim,), (right_dim,)), ((), ())),...  90.4 us
    psum x2, blocking collectives, section_whole(): factor = inverse_factor(lax.psum(product(panel, panel, 1, 1), 'rows'))  86.7 us
    reduce_sum x2, other arithmetic, on_device(): panel = lax.all_gather(partial_value, 'snaps').sum(axis=0)  18.5 us
    another operation x6, other arithmetic, inverse_factor(): lower = jnp.linalg.cholesky(gram_total)  13 us
  transfers between devices with their start and end apart: 4, of which 4 were waited for; matrix products, arithmetic and copies ran while one was open for 0% of the time, Pallas kernels for 0%

profile of v1, /device:TPU:0, one launch (start us, length us, event | category | flops | bytes accessed | tf_op | source)
XLA Modules:
  0.0 594.5 jit_solution(1053675495872672289)
XLA Ops:
  7.2 0.0 copy-start
  7.2 0.0 all-gather.5.cloned.1.call-start
  7.2 0.8 copy-done
  8.0 20.6 %fusion.12 = f32[64,16384]{1,0:T(8,128)} fusion(f32[64,256]{1,0:T(8,128)S(1)} %copy-done, f32[16384,256]{1,0:T(8,128)} %param.5), kind=kOutput, calls=%fused_computation.23 | convolution fusion | flops 3221225472 | bytes 21037056 | tf_op jit(solution)/shard_map/dot_general | solution.py:9
  28.6 0.0 all-gather.5.cloned.1.call-update
  28.7 0.0 all-reduce.3.cloned.1.call-start
  28.7 108.7 %all-gather.5.cloned.1.call-done = f32[256,16384]{1,0:T(8,128)} async-done(((f32[64,16384]{1,0:T(8,128)}), f32[256,16384]{1,0:T(8,128)}) %all-gather.5.cloned.1.call-update) | async-done | bytes 16777232 | tf_op jit(solution)/shard_map/all_gather | solution.py:39
  137.4 9.2 %reduce_sum.18 = f32[64,16384]{1,0:T(8,128)} reduce(f32[4,64,16384]{2,1,0:T(8,128)} %bitcast.39, f32[]{:T(128)} %constant.39.clone.1), dimensions={0}, to_apply=%region_0.0 | reduce | flops 3145728 | bytes 20971524 | tf_op jit(solution)/shard_map/reduce_sum | solution.py:39
  146.7 6.9 %fusion.13 = f32[64,64]{0,1:T(8,128)S(1)} fusion(f32[64,16384]{1,0:T(8,128)} %reduce_sum.18), kind=kOutput, calls=%fused_computation.24 | convolution fusion | flops 805306368 | bytes 4210688 | tf_op jit(solution)/shard_map/dot_general | solution.py:9
  153.6 49.6 %psum.35 = f32[64,64]{0,1:T(8,128)S(1)} all-reduce(f32[64,64]{0,1:T(8,128)S(1)} %fusion.13), channel_id=1, replica_groups=mesh['rows'=8,'snaps'=4] {'rows'}, use_global_device_ids=true, to_apply=%region_1.0 | all-reduce | flops 4096 | bytes 32768 | tf_op jit(solution)/shard_map/psum | solution.py:25
  203.2 0.1 copy.6
  203.3 5.8 cholesky.44
  209.1 0.6 compare_reduce_fusion.1
  209.8 0.7 fusion.4
  210.5 4.9 custom-call.6
  215.3 0.3 fusion.2
  215.6 5.5 fusion.14
  221.1 11.6 %fusion.15 = f32[64,256]{1,0:T(8,128)} fusion(f32[64,16384]{1,0:T(8,128)S(1)} %fusion.14, f32[16384,256]{1,0:T(8,128)} %param.5), kind=kOutput, calls=%fused_computation.26 | convolution fusion | flops 3221225472 | bytes 21037056 | tf_op jit(solution)/shard_map/dot_general | solution.py:9
  232.7 0.0 all-reduce.3.cloned.1.call-update
  232.7 0.0 all-gather.7.cloned.1.call-start
  232.7 64.9 %all-reduce.3.cloned.1.call-done = f32[64,256]{1,0:T(8,128)} async-done(((f32[64,256]{1,0:T(8,128)}), f32[64,256]{1,0:T(8,128)}) %all-reduce.3.cloned.1.call-update) | async-done | bytes 65552 | tf_op jit(solution)/shard_map/psum | solution.py:27
  297.7 20.6 %fusion.16 = f32[64,16384]{1,0:T(8,128)} fusion(f32[64,256]{1,0:T(8,128)} %all-reduce.3.cloned.1.call-done, f32[16384,256]{1,0:T(8,128)} %param.5), kind=kOutput, calls=%fused_computation.27 | convolution fusion | flops 3221225472 | bytes 21037056 | tf_op jit(solution)/shard_map/dot_general | solution.py:9
  318.3 0.0 all-gather.7.cloned.1.call-update
  318.3 0.0 all-reduce.5.cloned.1.call-start
  318.4 106.0 %all-gather.7.cloned.1.call-done = f32[256,16384]{1,0:T(8,128)} async-done(((f32[64,16384]{1,0:T(8,128)}), f32[256,16384]{1,0:T(8,128)}) %all-gather.7.cloned.1.call-update) | async-done | bytes 16777232 | tf_op jit(solution)/shard_map/all_gather | solution.py:39
  424.3 9.2 %reduce_sum.19 = f32[64,16384]{1,0:T(8,128)} reduce(f32[4,64,16384]{2,1,0:T(8,128)} %bitcast.38, f32[]{:T(128)} %constant.39.clone.1), dimensions={0}, to_apply=%region_5.8 | reduce | flops 3145728 | bytes 20971524 | tf_op jit(solution)/shard_map/reduce_sum | solution.py:39
  433.5 6.9 %fusion.17 = f32[64,64]{0,1:T(8,128)S(1)} fusion(f32[64,16384]{1,0:T(8,128)} %reduce_sum.19), kind=kOutput, calls=%fused_computation.28 | convolution fusion | flops 805306368 | bytes 4210688 | tf_op jit(solution)/shard_map/dot_general | solution.py:9
  440.5 37.1 %psum.37 = f32[64,64]{0,1:T(8,128)S(1)} all-reduce(f32[64,64]{0,1:T(8,128)S(1)} %fusion.17), channel_id=1, replica_groups=mesh['rows'=8,'snaps'=4] {'rows'}, use_global_device_ids=true, to_apply=%region_6.9 | all-reduce | flops 4096 | bytes 32768 | tf_op jit(solution)/shard_map/psum | solution.py:25
  477.6 0.1 copy.8
  477.7 5.8 cholesky.55
  483.6 0.6 compare_reduce_fusion
  484.2 0.7 fusion.5
  484.9 4.9 custom-call.7
  489.8 0.3 fusion
  490.1 5.5 fusion.18
  495.5 0.0 copy-start.2
  495.5 1.9 copy-done.2
  497.5 0.0 copy-start.1
  497.5 11.6 %fusion.19 = f32[64,256]{1,0:T(8,128)} fusion(f32[64,16384]{1,0:T(8,128)S(1)} %fusion.18, f32[16384,256]{1,0:T(8,128)} %param.5), kind=kOutput, calls=%fused_computation.30 | convolution fusion | flops 3221225472 | bytes 21037056 | tf_op jit(solution)/shard_map/dot_general | solution.py:9
  509.1 0.0 all-reduce.5.cloned.1.call-update
  509.1 2.3 dynamic-slice_multiply_fusion
  511.4 62.7 %all-reduce.5.cloned.1.call-done = f32[64,256]{1,0:T(8,128)} async-done(((f32[64,256]{1,0:T(8,128)}), f32[64,256]{1,0:T(8,128)}) %all-reduce.5.cloned.1.call-update) | async-done | bytes 65552 | tf_op jit(solution)/shard_map/psum | solution.py:27
  574.1 1.1 fusion.20
  575.2 10.3 %psum.39 = f32[64,64]{1,0:T(8,128)S(1)} all-reduce(f32[64,64]{1,0:T(8,128)S(1)} %fusion.20), channel_id=1, replica_groups=mesh['rows'=8,'snaps'=4] {'snaps'}, use_global_device_ids=true, to_apply=%region_8.11 | all-reduce | flops 4096 | bytes 32768 | tf_op jit(solution)/shard_map/psum | solution.py:44
  585.5 0.6 broadcast_multiply_fusion
  586.1 1.5 copy.13
  587.6 0.0 copy-done.1
  (4 shorter events, 0.1 us)
Async XLA Ops:
  7.2 0.8 copy-start
  7.2 130.3 %all-gather.5.cloned.1.call-start = ((), (), s32[]{:S(2)}) async-start(), calls=%async_computation.2 | async-start | bytes 20971520 | tf_op jit(solution)/shard_map/all_gather | solution.py:39
  28.7 269.0 %all-reduce.3.cloned.1.call-start = ((), (), s32[]{:S(2)}) async-start(), calls=%async_computation | async-start | bytes 131072 | tf_op jit(solution)/shard_map/psum | solution.py:27
  232.7 191.6 %all-gather.7.cloned.1.call-start = ((), (), s32[]{:S(2)}) async-start(), calls=%async_computation.3 | async-start | bytes 20971520 | tf_op jit(solution)/shard_map/all_gather | solution.py:39
  318.3 255.8 %all-reduce.5.cloned.1.call-start = ((), (), s32[]{:S(2)}) async-start(), calls=%async_computation.1 | async-start | bytes 131072 | tf_op jit(solution)/shard_map/psum | solution.py:27
  495.5 1.9 copy-start.2
  497.5 90.1 %copy-start.1 = (f32[64,256]{1,0:T(8,128)S(1)}, f32[64,256]{1,0:T(8,128)}, u32[]{:S(2)}) copy-start(f32[64,256]{1,0:T(8,128)} %param.6) | copy-start | bytes 196612
Sparse Core Ops, SparseCore 0:
  28.8 108.6 all-gather.4
  232.8 64.7 all-reduce.2
  318.4 105.8 all-gather.6
  509.2 64.8 all-reduce.4
